TPU v7x, 32 devices: a whole 2x2x4 slice. The times are simulated.
32 devices in a mesh: basin: 8 (over z, x), event: 4 (over y, core).
Axes of the slice: x: 2, y: 2, z: 4, core: 2. Of those that a mesh axis runs over, the one named last changes fastest.
Arguments:
- reach_attrs: bfloat16 [12288, 32], P('basin'), may hold values from -6 to 6
- w_first: bfloat16 [32, 768], replicated, may hold values from -1 to 1
- b_first: float32 [768], replicated, may hold values from -3 to 3
- w_second: bfloat16 [768, 768], replicated, may hold values from -0.21875 to 0.21875
- b_second: float32 [768], replicated, may hold values from -3 to 3
- w_out: bfloat16 [768], replicated, may hold values from -0.21875 to 0.21875
- section_factor: float32 [10], replicated, may hold values from 0.5 to 2
- bed_slope: float32 [12288], P('basin'), may hold values from 0.0001 to 0.004
- seg_count: int32 [12288], P('basin'), may hold values from 1 to 8
- section_class: int32 [12288], P('basin'), may hold values from 0 to 9
- down_local: int32 [12288], P('basin'), may hold values from 0 to 1536, as said below
- send_list: int32 [8, 8, 24], P('basin'), may hold values from 0 to 1536, as said below
- recv_list: int32 [8, 8, 24], P('basin'), may hold values from 0 to 1536, as said below
- area_start: float32 [128, 12288], P('event', 'basin'), may hold values from 0.2 to 2
- lateral: float32 [3, 128, 12288], P(None, 'event', 'basin'), may hold values from 0.05 to 1
- cotangent: float32 [128, 12288], P('event', 'basin'), may hold values from -6 to 6
Outputs:
- outflow: float32 [128, 12288], P('event', 'basin')
- grad_lateral: float32 [3, 128, 12288], P(None, 'event', 'basin')
- grad_w_first: float32 [32, 768], replicated
- grad_b_first: float32 [768], replicated
- grad_w_second: float32 [768, 768], replicated
- grad_b_second: float32 [768], replicated
- grad_w_out: float32 [768], replicated
Inputs may be any that keep to these rules, and one draw needn't show every extreme that they name: `down_local`: the downstream reach of a reach in its own sub-basin, as a local index 1 to 8 above the reach's own; 1536 where the reach drains into another sub-basin (it is then listed in send_list) or leaves the network. send_list[s, d, c] is a local reach of sub-basin s whose end flow enters sub-basin d, or 1536 for an empty slot; live slots come first in each list and no reach is listed twice. Only the lists from s to (s + 1), (s + 2), (s + 4) and (s + 7) mod 8 can hold live slots; those to (s + 1), (s + 4) and (s + 7) are always full, the one to (s + 2) is empty or holds 12 or more. One sub-basin receives 24 from each of the four sub-basins that can drain into it. recv_list[d, s, c] is the local reach of sub-basin d that receives slot c of send_list[s, d], and is 1536 exactly where that slot is empty; no reach is a target twice.
All inputs are finite; a program needn't handle non-finite values.
Results may differ from a plain program's by a relative error of at most 0.02.
Values sent between devices are 32-bit elements; how exact they have to be, the bound alone decides.
A program may use at most 64 MiB of HBM per device.

v0:
```python
import math
import jax
import jax.numpy as jnp
from jax import lax
from jax.sharding import PartitionSpec as P

STEPS = 3


def emit(area_now, flow_rate):
    return flow_rate * area_now ** (5.0 / 3.0)


def advance(area_now, inflow, lateral_now, flow_rate, beta_step):
    return (area_now + beta_step * (inflow + lateral_now)) / (
        1.0 + beta_step * flow_rate * area_now ** (2.0 / 3.0)
    )


def network_forward(reach_attrs, w_first, b_first, w_second, b_second, w_out):
    tanh_one = jnp.tanh(jnp.dot(reach_attrs, w_first, preferred_element_type=jnp.float32) + b_first)
    hid_one = tanh_one.astype(jnp.bfloat16)
    tanh_two = jnp.tanh(jnp.dot(hid_one, w_second, preferred_element_type=jnp.float32) + b_second)
    hid_two = tanh_two.astype(jnp.bfloat16)
    squash = jax.nn.sigmoid(jnp.dot(hid_two, w_out, preferred_element_type=jnp.float32))
    return (0.02 + 0.08 * squash, (tanh_one, hid_one, tanh_two, hid_two, squash))


def upper_grads(saved_acts, w_out, g_rough, scale):
    tanh_one, hid_one, tanh_two, hid_two, squash = saved_acts
    g_logit = (g_rough * scale * 0.08 * squash * (1.0 - squash)).astype(jnp.bfloat16)
    grad_w_out = jnp.dot(g_logit, hid_two, preferred_element_type=jnp.float32)
    g_pre_two = (
        g_logit.astype(jnp.float32)[:, None]
        * w_out.astype(jnp.float32)[None, :]
        * (1.0 - tanh_two * tanh_two)
    )
    g_two = g_pre_two.astype(jnp.bfloat16)
    grad_w_second = jnp.dot(hid_one.T, g_two, preferred_element_type=jnp.float32)
    return (g_two, (grad_w_out, jnp.sum(g_pre_two, axis=0), grad_w_second))


def lower_grads(reach_attrs, w_second, saved_acts, g_two):
    tanh_one = saved_acts[0]
    g_pre_one = jnp.dot(g_two, w_second.T, preferred_element_type=jnp.float32) * (
        1.0 - tanh_one * tanh_one
    )
    grad_w_first = jnp.dot(
        reach_attrs.T, g_pre_one.astype(jnp.bfloat16), preferred_element_type=jnp.float32
    )
    return (jnp.sum(g_pre_one, axis=0), grad_w_first)


def body(
    reach_attrs,
    w_first,
    b_first,
    w_second,
    b_second,
    w_out,
    section_factor,
    bed_slope,
    seg_count,
    section_class,
    down_local,
    send_list,
    recv_list,
    area_start,
    lateral,
    cotangent,
):
    local_events, local_reaches = area_start.shape
    class_total = section_factor.shape[0]
    one_hot = (section_class[:, None] == jnp.arange(class_total, dtype=jnp.int32)[None, :]).astype(
        jnp.float32
    )
    k_base = jnp.sqrt(bed_slope) * jnp.sum(one_hot * section_factor[None, :], axis=1)
    beta_step = 1.0 / seg_count.astype(jnp.float32)
    senders = send_list.reshape(-1)
    targets = recv_list.reshape(-1)
    zero_column = jnp.zeros((local_events, 1), jnp.float32)
    roughness, saved_acts = network_forward(
        reach_attrs, w_first, b_first, w_second, b_second, w_out
    )

    def rate_of(rough_all):
        return k_base / rough_all

    flow_rate, pull_rate = jax.vjp(rate_of, roughness)

    def step_of(area_now, inflow, lateral_now, rate_now):
        return advance(area_now, inflow, lateral_now, rate_now, beta_step)

    areas = [area_start]
    inflows = []
    flow_now = emit(area_start, flow_rate)
    for step in range(STEPS):
        confluence_padded = jnp.concatenate([flow_now, zero_column], axis=1)
        confluence_inflow = (
            jnp.zeros((local_events, local_reaches + 1), jnp.float32)
            .at[:, down_local]
            .add(flow_now)
        )
        arrived = lax.all_to_all(
            confluence_padded[:, senders], "basin", split_axis=1, concat_axis=1, tiled=True
        )
        confluence_inflow = confluence_inflow.at[:, targets].add(arrived)
        inflow = confluence_inflow[:, :local_reaches]
        inflows.append(inflow)
        area_next = step_of(areas[step], inflow, lateral[step], flow_rate)
        areas.append(area_next)
        flow_now = emit(area_next, flow_rate)
    g_area, g_rate = jax.vjp(emit, areas[STEPS], flow_rate)[1](cotangent)
    grads_lat = [None] * STEPS
    for step in reversed(range(STEPS)):
        g_prev, g_inflow, g_lateral, g_rate_step = jax.vjp(
            step_of, areas[step], inflows[step], lateral[step], flow_rate
        )[1](g_area)
        grads_lat[step] = g_lateral
        padded = jnp.concatenate([g_inflow, zero_column], axis=1)
        g_flow = jnp.zeros((local_events, local_reaches + 1), jnp.float32)
        returned = lax.all_to_all(
            padded[:, targets], "basin", split_axis=1, concat_axis=1, tiled=True
        )
        g_flow = g_flow.at[:, senders].add(returned)
        g_flow = g_flow[:, :local_reaches] + padded[:, down_local]
        g_emit_area, g_emit_rate = jax.vjp(emit, areas[step], flow_rate)[1](g_flow)
        g_area = g_prev + g_emit_area
        g_rate = g_rate + g_rate_step + g_emit_rate
    grad_lateral = jnp.stack(grads_lat, axis=0)
    g_rough = pull_rate(g_rate)[0]
    scale = 32.0 / math.sqrt(
        local_events * lax.axis_size("event") * local_reaches * lax.axis_size("basin")
    )
    g_two, upper = upper_grads(saved_acts, w_out, g_rough, scale)
    upper = lax.psum((upper[0], upper[1], upper[2]), ("basin", "event"))
    lower = lax.psum(lower_grads(reach_attrs, w_second, saved_acts, g_two), ("basin", "event"))
    grad_w_out, grad_b_second, grad_w_second = upper
    grad_b_first, grad_w_first = lower
    return (
        flow_now,
        grad_lateral,
        grad_w_first,
        grad_b_first,
        grad_w_second,
        grad_b_second,
        grad_w_out,
    )


def solution(mesh):
    return jax.shard_map(
        body,
        mesh=mesh,
        in_specs=(
            P("basin", None),
            P(),
            P(),
            P(),
            P(),
            P(),
            P(),
            P("basin"),
            P("basin"),
            P("basin"),
            P("basin"),
            P("basin", None, None),
            P("basin", None, None),
            P("event", "basin"),
            P(None, "event", "basin"),
            P("event", "basin"),
        ),
        out_specs=(P("event", "basin"), P(None, "event", "basin"), P(), P(), P(), P(), P()),
        check_vma=False,
    )
```

profile of v0, /device:TPU:0, one launch (start us, length us, event | category | flops | bytes accessed | tf_op | source)
XLA Modules:
  0.0 334.1 jit_solution(14651421957676418809)
XLA Ops:
  8.0 1.7 fusion.52
  9.9 2.1 fusion.13
  12.0 2.1 copy-done.1
  18.8 7.3 %all-to-all-start = ((f32[8,1,768]{2,1,0:T(1,128)}), f32[8,1,768]{2,1,0:T(1,128)}, u32[]{:S(2)}, u32[]{:S(2)}) async-start(f32[8,1,768]{2,1,0:T(1,128)} %reshape.288), calls=%async_computation | async-start | bytes 49152 | tf_op jit(solution)/shard_map/all_to_all | solution.py:104
  29.0 9.0 %scatter_custom_fusion = f32[32,1537]{0,1:T(8,128)S(1)} fusion(s32[1536]{0:T(1024)} %compare_select_fusion, f32[1536,32]{1,0:T(8,128)S(1)} %copy.57, f32[]{:T(128)} %constant.11.clone.1), kind=kCustom, calls=%fused_computation.44 | custom fusion | flops 49152 | bytes 197248 | tf_op jit(solution)/shard_map/scatter-add | solution.py:102
  38.6 1.4 reduce.4
  40.1 2.0 scatter_fusion
  42.5 1.8 power_multiply_fusion.2
  45.5 2.0 gather_fusion.1
  48.2 6.1 %all-to-all-start.1 = ((f32[8,1,768]{2,1,0:T(1,128)}), f32[8,1,768]{2,1,0:T(1,128)S(1)}, u32[]{:S(2)}, u32[]{:S(2)}) async-start(f32[8,1,768]{2,1,0:T(1,128)} %reshape.290), calls=%async_computation.1 | async-start | bytes 49152 | tf_op jit(solution)/shard_map/all_to_all | solution.py:104
  55.4 9.3 %scatter_custom_fusion.2 = f32[32,1537]{0,1:T(8,128)S(1)} fusion(s32[1536]{0:T(1024)} %compare_select_fusion, f32[1536,32]{1,0:T(8,128)} %copy.60, f32[]{:T(128)} %constant.11.clone.1), kind=kCustom, calls=%fused_computation.42 | custom fusion | flops 49152 | bytes 197248 | tf_op jit(solution)/shard_map/scatter-add | solution.py:102
  65.5 2.1 scatter_fusion.1
  68.0 1.4 power_multiply_fusion.1
  70.6 2.0 gather_fusion.2
  73.3 6.1 %all-to-all-start.2 = ((f32[8,1,768]{2,1,0:T(1,128)}), f32[8,1,768]{2,1,0:T(1,128)S(1)}, u32[]{:S(2)}, u32[]{:S(2)}) async-start(f32[8,1,768]{2,1,0:T(1,128)} %reshape.292), calls=%async_computation.2 | async-start | bytes 49152 | tf_op jit(solution)/shard_map/all_to_all | solution.py:104
  81.8 9.3 %scatter_custom_fusion.4 = f32[32,1537]{0,1:T(8,128)S(1)} fusion(s32[1536]{0:T(1024)} %compare_select_fusion, f32[1536,32]{1,0:T(8,128)} %copy.63, f32[]{:T(128)} %constant.11.clone.1), kind=kCustom, calls=%fused_computation.40 | custom fusion | flops 49152 | bytes 197248 | tf_op jit(solution)/shard_map/scatter-add | solution.py:102
  91.9 2.0 scatter_fusion.2
  94.8 1.4 copy.80
  100.3 1.4 gather_fusion.3
  101.7 1.6 reshape.294
  103.3 6.1 %all-to-all-start.3 = ((f32[8,1,768]{2,1,0:T(1,128)}), f32[8,1,768]{2,1,0:T(1,128)}, u32[]{:S(2)}, u32[]{:S(2)}) async-start(f32[8,1,768]{2,1,0:T(1,128)} %reshape.294), calls=%async_computation.3 | async-start | bytes 49152 | tf_op jit(solution)/shard_map/all_to_all | solution.py:122
  110.7 4.0 %gather_fusion.4 = f32[1536,32]{1,0:T(8,128)} fusion(f32[32,1537]{0,1:T(8,128)S(1)} %concatenate.21.clone, s32[2048]{0:T(1024)} %pad_clamp_fusion), kind=kCustom, calls=%fused_computation.4 | custom fusion | bytes 399360 | tf_op jit(solution)/shard_map/gather | solution.py:126
  114.7 2.0 copy.69
  116.8 1.4 reduce.7
  118.9 2.1 scatter_custom_fusion.6
  122.0 1.4 copy.81
  123.3 3.3 fusion.41
  129.6 1.4 gather_fusion.5
  131.1 1.6 reshape.296
  132.6 5.9 %all-to-all-start.4 = ((f32[8,1,768]{2,1,0:T(1,128)}), f32[8,1,768]{2,1,0:T(1,128)}, u32[]{:S(2)}, u32[]{:S(2)}) async-start(f32[8,1,768]{2,1,0:T(1,128)} %reshape.296), calls=%async_computation.4 | async-start | bytes 49152 | tf_op jit(solution)/shard_map/all_to_all | solution.py:122
  138.6 4.0 %gather_fusion.6 = f32[1536,32]{1,0:T(8,128)} fusion(f32[32,1537]{0,1:T(8,128)S(1)} %concatenate.22.clone, s32[2048]{0:T(1024)} %pad_clamp_fusion), kind=kCustom, calls=%fused_computation.6 | custom fusion | bytes 399360 | tf_op jit(solution)/shard_map/gather | solution.py:126
  142.6 2.1 copy.73
  145.3 1.4 reduce.8
  147.5 2.3 scatter_custom_fusion.7
  150.7 1.4 copy.82
  152.1 3.2 multiply_reduce_fusion.4
  158.3 5.3 %all-to-all-start.5 = ((f32[8,1,768]{2,1,0:T(1,128)}), f32[8,1,768]{2,1,0:T(1,128)S(1)}, u32[]{:S(2)}, u32[]{:S(2)}) async-start(f32[8,1,768]{2,1,0:T(1,128)} %reshape.298), calls=%async_computation.5 | async-start | bytes 49152 | tf_op jit(solution)/shard_map/all_to_all | solution.py:122
  164.3 3.0 gather_fusion.8
  167.6 2.7 all-to-all-done.5
  171.0 1.9 scatter_custom_fusion.8
  173.5 7.0 %fusion.51 = (f32[768]{0:T(1024)S(1)}, bf16[1536,768]{1,0:T(8,128)(2,1)S(1)}) fusion(f32[1536,768]{1,0:T(8,128)} %copy-done.3, f32[768]{0:T(1024)S(1)} %copy-done.37, bf16[768,768]{1,0:T(8,128)(2,1)S(1)} %copy-done, f32[1536,768]{1,0:T(8,128)} %copy-done.1, f32[768]{0:T(1024)S(1)} %convert_element_type.30, f32[1536]{0:T(1024)S(1)} %get-tuple-element.38, ...), kind=kOutput, calls=%fused_computation.102 | convolution fusion | flops 1826094336 | bytes 12994560 | tf_op jit(solution)/shard_map/dot_general | solution.py:45
  180.6 6.2 %fusion.11 = f32[768,768]{1,0:T(8,128)} fusion(f32[1536,768]{1,0:T(8,128)} %copy-done.3, f32[768]{0:T(1024)S(1)} %copy-done.37, f32[1536,768]{1,0:T(8,128)S(1)} %bitcast.127, f32[768]{0:T(1024)S(1)} %convert_element_type.30, f32[1536]{0:T(1024)S(1)} %get-tuple-element.38, f32[768]{0:T(1024)S(1)} %copy-done.20), kind=kOutput, calls=%fused_computation.31 | convolution fusion | flops 1821376512 | bytes 11811840 | tf_op jit(solution)/shard_map/dot_general | solution.py:39
  188.8 3.1 convolution_reduce_fusion.1
  191.9 3.6 %fusion.2 = f32[768]{0:T(1024)S(1)} fusion(f32[1536,768]{1,0:T(8,128)} %copy-done.1, f32[768]{0:T(1024)S(1)} %convert_element_type.30, f32[1536]{0:T(1024)S(1)} %get-tuple-element.38, f32[768]{0:T(1024)S(1)} %copy-done.20), kind=kLoop, calls=%fused_computation.24 | loop fusion | flops 7077120 | bytes 4733952 | tf_op jit(solution)/shard_map/reduce_sum | solution.py:40
  195.4 38.7 %all-reduce.6 = (f32[768]{0:T(1024)}, f32[768]{0:T(1024)}, f32[768]{0:T(1024)}) all-reduce(f32[768]{0:T(1024)S(1)} %get-tuple-element.54, f32[768]{0:T(1024)S(1)} %fusion.2, f32[768]{0:T(1024)S(1)} %convolution_reduce_fusion.1), channel_id=1, replica_groups=mesh['basin'=8,'event'=4] {'basin','event'}, use_global_device_ids=true, to_apply=%region_19.0 | all-reduce | flops 2304 | bytes 18432 | tf_op jit(solution)/shard_map/psum | solution.py:137
  234.2 88.4 %all-reduce.10.cloned.1.call-done = (f32[32,768]{1,0:T(8,128)}, f32[768,768]{1,0:T(8,128)}) async-done(((f32[32,768]{1,0:T(8,128)}, f32[768,768]{1,0:T(8,128)}), (f32[32,768]{1,0:T(8,128)}, f32[768,768]{1,0:T(8,128)})) %all-reduce.10.cloned.1.call-update) | async-done | bytes 2457616 | tf_op jit(solution)/shard_map/psum | solution.py:137
  322.5 1.5 copy.95
  324.1 3.2 copy.96
  (150 shorter events, 39.1 us)
Async XLA Ops:
  7.2 2.7 copy-start
  7.2 2.5 copy-start.35
  7.2 2.5 copy-start.32
  7.2 2.6 copy-start.36
  9.7 2.2 copy-start.3
  9.8 5.0 %copy-start.18 = (f32[1536]{0:T(1024)}, f32[1536]{0:T(1024)S(1)}, u32[]{:S(2)}) copy-start(f32[1536]{0:T(1024)S(1)} %select_reduce_fusion) | copy-start | bytes 18436
  9.9 4.2 %copy-start.20 = (f32[768]{0:T(1024)S(1)}, f32[768]{0:T(1024)}, u32[]{:S(2)}) copy-start(f32[768]{0:T(1024)} %param.20) | copy-start | bytes 9220
  11.9 2.1 copy-start.1
  14.1 0.8 copy-start.27
  14.1 0.8 copy-start.29
  14.1 1.5 copy-start.2
  14.1 1.8 copy-start.33
  14.9 0.6 copy-start.16
  14.9 27.6 %copy-start.4 = (f32[3,32,1536]{2,1,0:T(8,128)S(1)}, f32[3,32,1536]{2,1,0:T(8,128)}, u32[]{:S(2)}) copy-start(f32[3,32,1536]{2,1,0:T(8,128)} %param.30) | copy-start | bytes 1769476
  16.0 0.6 copy-start.34
  18.8 19.3 %all-to-all-start = ((f32[8,1,768]{2,1,0:T(1,128)}), f32[8,1,768]{2,1,0:T(1,128)}, u32[]{:S(2)}, u32[]{:S(2)}) async-start(f32[8,1,768]{2,1,0:T(1,128)} %reshape.288), calls=%async_computation | async-start | bytes 49152 | tf_op jit(solution)/shard_map/all_to_all | solution.py:104
  42.5 1.8 copy-start.11
  42.5 23.0 %copy-start.31 = (s32[192,1]{0,1:T(1,128)S(1)}, s32[192,1]{0,1:T(1,128)}, u32[]{:S(2)}) copy-start(s32[192,1]{0,1:T(1,128)} %compare_select_fusion.2) | copy-start | bytes 2308
  48.2 16.5 %all-to-all-start.1 = ((f32[8,1,768]{2,1,0:T(1,128)}), f32[8,1,768]{2,1,0:T(1,128)S(1)}, u32[]{:S(2)}, u32[]{:S(2)}) async-start(f32[8,1,768]{2,1,0:T(1,128)} %reshape.290), calls=%async_computation.1 | async-start | bytes 49152 | tf_op jit(solution)/shard_map/all_to_all | solution.py:104
  67.9 1.4 copy-start.12
  67.9 28.3 %copy-start.6 = (f32[32,1536]{1,0:T(8,128)S(1)}, f32[32,1536]{1,0:T(8,128)}, u32[]{:S(2)}) copy-start(f32[32,1536]{1,0:T(8,128)} %param.31) | copy-start | bytes 589828
  67.9 28.3 %copy-start.13 = (f32[1536]{0:T(1024)S(1)}, f32[1536]{0:T(1024)}, u32[]{:S(2)}) copy-start(f32[1536]{0:T(1024)} %get-tuple-element.49) | copy-start | bytes 18436
  67.9 28.3 %copy-start.14 = (f32[1536]{0:T(1024)S(1)}, f32[1536]{0:T(1024)}, u32[]{:S(2)}) copy-start(f32[1536]{0:T(1024)} %get-tuple-element.53) | copy-start | bytes 18436
  73.3 17.8 %all-to-all-start.2 = ((f32[8,1,768]{2,1,0:T(1,128)}), f32[8,1,768]{2,1,0:T(1,128)S(1)}, u32[]{:S(2)}, u32[]{:S(2)}) async-start(f32[8,1,768]{2,1,0:T(1,128)} %reshape.292), calls=%async_computation.2 | async-start | bytes 49152 | tf_op jit(solution)/shard_map/all_to_all | solution.py:104
  97.3 0.7 copy-start.7
  97.3 26.1 %copy-start.5 = (f32[32,1536]{1,0:T(8,128)S(1)}, f32[32,1536]{1,0:T(8,128)}, u32[]{:S(2)}) copy-start(f32[32,1536]{1,0:T(8,128)} %get-tuple-element.48) | copy-start | bytes 589828
  103.3 13.4 %all-to-all-start.3 = ((f32[8,1,768]{2,1,0:T(1,128)}), f32[8,1,768]{2,1,0:T(1,128)}, u32[]{:S(2)}, u32[]{:S(2)}) async-start(f32[8,1,768]{2,1,0:T(1,128)} %reshape.294), calls=%async_computation.3 | async-start | bytes 49152 | tf_op jit(solution)/shard_map/all_to_all | solution.py:122
  126.6 0.7 copy-start.9
  132.6 12.7 %all-to-all-start.4 = ((f32[8,1,768]{2,1,0:T(1,128)}), f32[8,1,768]{2,1,0:T(1,128)}, u32[]{:S(2)}, u32[]{:S(2)}) async-start(f32[8,1,768]{2,1,0:T(1,128)} %reshape.296), calls=%async_computation.4 | async-start | bytes 49152 | tf_op jit(solution)/shard_map/all_to_all | solution.py:122
  156.6 16.8 %copy-start.17 = (f32[1536]{0:T(1024)S(1)}, f32[1536]{0:T(1024)}, u32[]{:S(2)}) copy-start(f32[1536]{0:T(1024)} %copy-done.16) | copy-start | bytes 18436
  156.6 16.8 %copy-start.19 = (f32[1536]{0:T(1024)S(1)}, f32[1536]{0:T(1024)}, u32[]{:S(2)}) copy-start(f32[1536]{0:T(1024)} %copy-done.18) | copy-start | bytes 18436
  156.6 16.8 %copy-start.21 = (f32[1536]{0:T(1024)S(1)}, f32[1536]{0:T(1024)}, u32[]{:S(2)}) copy-start(f32[1536]{0:T(1024)} %get-tuple-element.51) | copy-start | bytes 18436
  156.6 16.8 %copy-start.22 = (f32[1536]{0:T(1024)S(1)}, f32[1536]{0:T(1024)}, u32[]{:S(2)}) copy-start(f32[1536]{0:T(1024)} %get-tuple-element.28) | copy-start | bytes 18436
  156.6 16.8 %copy-start.23 = (f32[1536]{0:T(1024)S(1)}, f32[1536]{0:T(1024)}, u32[]{:S(2)}) copy-start(f32[1536]{0:T(1024)} %get-tuple-element.29) | copy-start | bytes 18436
  156.6 16.8 %copy-start.24 = (f32[1536]{0:T(1024)S(1)}, f32[1536]{0:T(1024)}, u32[]{:S(2)}) copy-start(f32[1536]{0:T(1024)} %get-tuple-element.30) | copy-start | bytes 18436
  156.6 16.8 %copy-start.25 = (f32[1536]{0:T(1024)S(1)}, f32[1536]{0:T(1024)}, u32[]{:S(2)}) copy-start(f32[1536]{0:T(1024)} %get-tuple-element.31) | copy-start | bytes 18436
  156.6 16.8 %copy-start.26 = (f32[1536]{0:T(1024)S(1)}, f32[1536]{0:T(1024)}, u32[]{:S(2)}) copy-start(f32[1536]{0:T(1024)} %get-tuple-element.32) | copy-start | bytes 18436
  156.6 16.8 %copy-start.28 = (s32[1536]{0:T(1024)S(1)}, s32[1536]{0:T(1024)}, u32[]{:S(2)}) copy-start(s32[1536]{0:T(1024)} %param.24) | copy-start | bytes 18436
  156.7 16.8 %copy-start.30 = (f32[1536]{0:T(1024)S(1)}, f32[1536]{0:T(1024)}, u32[]{:S(2)}) copy-start(f32[1536]{0:T(1024)} %param.23) | copy-start | bytes 18436
  156.7 16.9 %copy-start.37 = (f32[768]{0:T(1024)S(1)}, f32[768]{0:T(1024)}, u32[]{:S(2)}) copy-start(f32[768]{0:T(1024)} %param.18) | copy-start | bytes 9220
  158.3 11.9 %all-to-all-start.5 = ((f32[8,1,768]{2,1,0:T(1,128)}), f32[8,1,768]{2,1,0:T(1,128)S(1)}, u32[]{:S(2)}, u32[]{:S(2)}) async-start(f32[8,1,768]{2,1,0:T(1,128)} %reshape.298), calls=%async_computation.5 | async-start | bytes 49152 | tf_op jit(solution)/shard_map/all_to_all | solution.py:122
  163.6 158.9 %all-reduce.10.cloned.1.call-start = ((), (), s32[]{:S(2)}) async-start(), calls=%async_computation.6 | async-start | bytes 4915200 | tf_op jit(solution)/shard_map/psum | solution.py:137
  173.0 7.5 %slice-start = ((s8[4718592]{0:T(1024)(128)(4,1)}), s8[524288]{0:T(1024)(128)(4,1)S(1)}, s32[]{:S(2)}) async-start(s8[4718592]{0:T(1024)(128)(4,1)} %bitcast.126), calls=%async_computation.7 | async-start | bytes 1048576
  173.5 7.0 %slice-start.1 = ((s8[4718592]{0:T(1024)(128)(4,1)}), s8[4194304]{0:T(1024)(128)(4,1)S(1)}, s32[]{:S(2)}) async-start(s8[4718592]{0:T(1024)(128)(4,1)} %bitcast.126), calls=%async_computation.8 | async-start | bytes 8388608
  180.5 6.2 %copy-start.15 = (bf16[1536,32]{0,1:T(8,128)(2,1)S(1)}, bf16[1536,32]{0,1:T(8,128)(2,1)}, u32[]{:S(2)}) copy-start(bf16[1536,32]{0,1:T(8,128)(2,1)} %param.16) | copy-start | bytes 294916
  186.7 1.2 copy-start.8
  186.7 1.2 copy-start.10
Sparse Core Ops, SparseCore 0:
  188.0 134.4 all-reduce.9
where the time goes:
time: 336 us; the launch traced here: 334 us
  waiting for transfers between devices  91.7 us (27%)
  other arithmetic  69.4 us (21%)
  local copies, waits for them, and re-layouts  60.8 us (18%)
  blocking collectives  38.7 us (12%)
  starting transfers between devices  36.8 us (11%)
  matrix products  21.9 us (7%)
  between operations  14.9 us (4%)
    psum x1, waiting for transfers between devices, body(): lax.psum(lower_grads(reach_attrs, w_second, saved_acts, g_two), ('basin',...  88.4 us
    psum x1, blocking collectives, body(): lax.psum(lower_grads(reach_attrs, w_second, saved_acts, g_two), ('basin',...  38.7 us
    scatter-add x3, other arithmetic, body(): confluence_inflow = jnp.zeros((local_events, local_reaches + 1), jnp.floa...  27.6 us
    unnamed x107, local copies, waits for them, and re-layouts  25.7 us
    all_to_all x3, starting transfers between devices, body(): lax.all_to_all(confluence_padded[:, senders], 'basin', split_axis=1, conc...  19.4 us
    all_to_all x3, starting transfers between devices, body(): lax.all_to_all(padded[:, targets], 'basin', split_axis=1, concat_axis=1,...  17.3 us
    gather x6, local copies, waits for them, and re-layouts, body(): g_flow = g_flow[:, :local_reaches] + padded[:, down_local]  15.3 us
    dot_general x1, matrix products, lower_grads(): jnp.dot(g_two, w_second.T, preferred_element_type=jnp.float32)  6.97 us
  transfers between devices with their start and end apart: 7, of which 3 were waited for; matrix products, arithmetic and copies ran while one was open for 18% of the time, Pallas kernels for 0%

commit v1 on v0

--- a/solution.py
+++ b/solution.py
@@ -134,7 +134,9 @@
     )
     g_two, upper = upper_grads(saved_acts, w_out, g_rough, scale)
     upper = lax.psum((upper[0], upper[1], upper[2]), ("basin", "event"))
-    lower = lax.psum(lower_grads(reach_attrs, w_second, saved_acts, g_two), ("basin", "event"))
+    lower = lax.psum(
+        lax.psum(lower_grads(reach_attrs, w_second, saved_acts, g_two), "event"), "basin"
+    )
     grad_w_out, grad_b_second, grad_w_second = upper
     grad_b_first, grad_w_first = lower
     return (

time: 336 us -> 441 us (1.31)
  waiting for transfers between devices: 91.7 us -> 166 us
  blocking collectives: 38.7 us -> 66.9 us
    psum x1 -> x3, waiting for transfers between devices: 88.4 us -> 163 us  [the longest x1 132 us: body(): upper = lax.psum((upper[0], upper[1], upper[2]), ('basin', 'event'))]
    psum x1 -> x3, blocking collectives: 38.7 us -> 66.9 us  [the longest x1 39.5 us: body(): upper = lax.psum((upper[0], upper[1], upper[2]), ('basin', 'event'))]
    unnamed x107 -> x87, local copies, waits for them, and re-layouts: 25.7 us -> 25.7 us
  transfers between devices with their start and end apart: 7 -> 9, of which waited for: 3 -> 4; matrix products, arithmetic and copies ran while one was open for 18% -> 15% of each run, Pallas kernels for 0% -> 0%
where the time goes in v1:
time: 441 us; the launch traced here: 439 us
  waiting for transfers between devices  166 us (38%)
  other arithmetic  70.5 us (16%)
  blocking collectives  66.9 us (15%)
  local copies, waits for them, and re-layouts  60.7 us (14%)
  starting transfers between devices  37.1 us (8%)
  matrix products  23.3 us (5%)
  between operations  14.4 us (3%)
    psum x1, waiting for transfers between devices, body(): upper = lax.psum((upper[0], upper[1], upper[2]), ('basin', 'event'))  132 us
    psum x1, blocking collectives, body(): upper = lax.psum((upper[0], upper[1], upper[2]), ('basin', 'event'))  39.5 us
    psum x1, waiting for transfers between devices, body(): lax.psum(lower_grads(reach_attrs, w_second, saved_acts, g_two), 'event')  30.7 us
    scatter-add x3, other arithmetic, body(): confluence_inflow = jnp.zeros((local_events, local_reaches + 1), jnp.floa...  27.6 us
    unnamed x87, local copies, waits for them, and re-layouts  25.7 us
    psum x1, blocking collectives, body(): lax.psum(lax.psum(lower_grads(reach_attrs, w_second, saved_acts, g_two),...  20.5 us
    all_to_all x3, starting transfers between devices, body(): lax.all_to_all(confluence_padded[:, senders], 'basin', split_axis=1, conc...  19.4 us
    all_to_all x3, starting transfers between devices, body(): lax.all_to_all(padded[:, targets], 'basin', split_axis=1, concat_axis=1,...  17.6 us
  transfers between devices with their start and end apart: 9, of which 4 were waited for; matrix products, arithmetic and copies ran while one was open for 15% of the time, Pallas kernels for 0%

profile of v1, /device:TPU:0, one launch (start us, length us, event | category | flops | bytes accessed | tf_op | source)
XLA Modules:
  0.0 438.6 jit_solution(7729788527165779916)
XLA Ops:
  8.0 1.7 fusion.52
  9.9 2.1 fusion.13
  12.0 2.1 copy-done.1
  18.8 7.3 %all-to-all-start = ((f32[8,1,768]{2,1,0:T(1,128)}), f32[8,1,768]{2,1,0:T(1,128)}, u32[]{:S(2)}, u32[]{:S(2)}) async-start(f32[8,1,768]{2,1,0:T(1,128)} %reshape.288), calls=%async_computation | async-start | bytes 49152 | tf_op jit(solution)/shard_map/all_to_all | solution.py:104
  29.0 9.0 %scatter_custom_fusion = f32[32,1537]{0,1:T(8,128)S(1)} fusion(s32[1536]{0:T(1024)} %compare_select_fusion, f32[1536,32]{1,0:T(8,128)S(1)} %copy.57, f32[]{:T(128)} %constant.11.clone.1), kind=kCustom, calls=%fused_computation.44 | custom fusion | flops 49152 | bytes 197248 | tf_op jit(solution)/shard_map/scatter-add | solution.py:102
  38.6 1.4 reduce.4
  40.1 2.0 scatter_fusion
  42.5 1.8 power_multiply_fusion.2
  45.5 2.0 gather_fusion.1
  48.2 6.1 %all-to-all-start.1 = ((f32[8,1,768]{2,1,0:T(1,128)}), f32[8,1,768]{2,1,0:T(1,128)S(1)}, u32[]{:S(2)}, u32[]{:S(2)}) async-start(f32[8,1,768]{2,1,0:T(1,128)} %reshape.290), calls=%async_computation.1 | async-start | bytes 49152 | tf_op jit(solution)/shard_map/all_to_all | solution.py:104
  55.4 9.3 %scatter_custom_fusion.2 = f32[32,1537]{0,1:T(8,128)S(1)} fusion(s32[1536]{0:T(1024)} %compare_select_fusion, f32[1536,32]{1,0:T(8,128)} %copy.60, f32[]{:T(128)} %constant.11.clone.1), kind=kCustom, calls=%fused_computation.42 | custom fusion | flops 49152 | bytes 197248 | tf_op jit(solution)/shard_map/scatter-add | solution.py:102
  65.5 2.1 scatter_fusion.1
  68.0 1.4 power_multiply_fusion.1
  70.6 2.0 gather_fusion.2
  73.3 6.1 %all-to-all-start.2 = ((f32[8,1,768]{2,1,0:T(1,128)}), f32[8,1,768]{2,1,0:T(1,128)S(1)}, u32[]{:S(2)}, u32[]{:S(2)}) async-start(f32[8,1,768]{2,1,0:T(1,128)} %reshape.292), calls=%async_computation.2 | async-start | bytes 49152 | tf_op jit(solution)/shard_map/all_to_all | solution.py:104
  81.8 9.3 %scatter_custom_fusion.4 = f32[32,1537]{0,1:T(8,128)S(1)} fusion(s32[1536]{0:T(1024)} %compare_select_fusion, f32[1536,32]{1,0:T(8,128)} %copy.63, f32[]{:T(128)} %constant.11.clone.1), kind=kCustom, calls=%fused_computation.40 | custom fusion | flops 49152 | bytes 197248 | tf_op jit(solution)/shard_map/scatter-add | solution.py:102
  91.9 2.0 scatter_fusion.2
  100.3 1.4 gather_fusion.3
  101.7 1.6 reshape.294
  103.3 6.1 %all-to-all-start.3 = ((f32[8,1,768]{2,1,0:T(1,128)}), f32[8,1,768]{2,1,0:T(1,128)}, u32[]{:S(2)}, u32[]{:S(2)}) async-start(f32[8,1,768]{2,1,0:T(1,128)} %reshape.294), calls=%async_computation.3 | async-start | bytes 49152 | tf_op jit(solution)/shard_map/all_to_all | solution.py:122
  110.7 4.0 gather_fusion.4
  114.7 2.0 copy.69
  116.8 1.4 reduce.7
  118.9 2.1 scatter_custom_fusion.6
  123.3 3.3 fusion.41
  129.6 1.4 gather_fusion.5
  131.1 1.6 reshape.296
  132.7 5.9 %all-to-all-start.4 = ((f32[8,1,768]{2,1,0:T(1,128)}), f32[8,1,768]{2,1,0:T(1,128)}, u32[]{:S(2)}, u32[]{:S(2)}) async-start(f32[8,1,768]{2,1,0:T(1,128)} %reshape.296), calls=%async_computation.4 | async-start | bytes 49152 | tf_op jit(solution)/shard_map/all_to_all | solution.py:122
  138.6 4.0 gather_fusion.6
  142.6 2.1 copy.73
  145.3 1.4 reduce.8
  147.5 2.1 scatter_custom_fusion.7
  151.9 3.2 multiply_reduce_fusion.4
  158.0 5.5 %all-to-all-start.5 = ((f32[8,1,768]{2,1,0:T(1,128)}), f32[8,1,768]{2,1,0:T(1,128)S(1)}, u32[]{:S(2)}, u32[]{:S(2)}) async-start(f32[8,1,768]{2,1,0:T(1,128)} %reshape.298), calls=%async_computation.5 | async-start | bytes 49152 | tf_op jit(solution)/shard_map/all_to_all | solution.py:122
  164.8 3.0 gather_fusion.8
  168.1 2.1 all-to-all-done.5
  170.9 1.9 scatter_custom_fusion.8
  174.2 6.9 %fusion.51 = (f32[768]{0:T(1024)S(1)}, bf16[1536,768]{1,0:T(8,128)(2,1)S(1)}) fusion(f32[1536,768]{1,0:T(8,128)} %copy-done.3, f32[768]{0:T(1024)} %param.18, bf16[768,768]{1,0:T(8,128)(2,1)S(1)} %copy-done, f32[1536,768]{1,0:T(8,128)} %copy-done.1, f32[768]{0:T(1024)} %convert_element_type.30, f32[1536]{0:T(1024)S(1)} %get-tuple-element.35, ...), kind=kOutput, calls=%fused_computation.102 | convolution fusion | flops 1826094336 | bytes 12994560 | tf_op jit(solution)/shard_map/dot_general | solution.py:45
  182.3 30.7 %all-reduce.11.cloned.1.call-done = f32[32,768]{1,0:T(8,128)} async-done(((f32[32,768]{1,0:T(8,128)}), f32[32,768]{1,0:T(8,128)}) %all-reduce.11.cloned.1.call-update) | async-done | bytes 98320 | tf_op jit(solution)/shard_map/psum | solution.py:138
  213.1 7.7 %fusion.11 = f32[768,768]{1,0:T(8,128)} fusion(f32[1536,768]{1,0:T(8,128)} %copy-done.3, f32[768]{0:T(1024)S(1)} %copy-done.29, f32[1536,768]{1,0:T(8,128)} %copy-done.1, f32[768]{0:T(1024)S(1)} %copy-done.23, f32[1536]{0:T(1024)S(1)} %get-tuple-element.35, f32[768]{0:T(1024)S(1)} %copy-done.19), kind=kOutput, calls=%fused_computation.31 | convolution fusion | flops 1821376512 | bytes 11811840 | tf_op jit(solution)/shard_map/dot_general | solution.py:39
  221.6 3.1 convolution_reduce_fusion.1
  224.7 3.5 fusion.2
  228.2 39.5 %all-reduce.6 = (f32[768]{0:T(1024)}, f32[768]{0:T(1024)}) all-reduce(f32[768]{0:T(1024)S(1)} %fusion.2, f32[768]{0:T(1024)S(1)} %convolution_reduce_fusion.1), channel_id=1, replica_groups=mesh['basin'=8,'event'=4] {'basin','event'}, use_global_device_ids=true, to_apply=%region_24.0 | all-reduce | flops 1536 | bytes 12288 | tf_op jit(solution)/shard_map/psum | solution.py:136
  267.7 6.8 %psum.51 = f32[768]{0:T(1024)S(1)} all-reduce(f32[768]{0:T(1024)S(1)} %get-tuple-element.51), channel_id=1, replica_groups=mesh['basin'=8,'event'=4] {'event'}, use_global_device_ids=true, to_apply=%region_20.0 | all-reduce | flops 768 | bytes 6144 | tf_op jit(solution)/shard_map/psum | solution.py:138
  274.5 20.5 %psum.52 = f32[768]{0:T(1024)} all-reduce(f32[768]{0:T(1024)S(1)} %psum.51), channel_id=1, replica_groups=mesh['basin'=8,'event'=4] {'basin'}, use_global_device_ids=true, to_apply=%region_21.0 | all-reduce | flops 768 | bytes 6144 | tf_op jit(solution)/shard_map/psum | solution.py:137
  295.0 132.2 %all-reduce.15.cloned.1.call-done = f32[768,768]{1,0:T(8,128)} async-done(((f32[768,768]{1,0:T(8,128)}), f32[768,768]{1,0:T(8,128)}) %all-reduce.15.cloned.1.call-update) | async-done | bytes 2359312 | tf_op jit(solution)/shard_map/psum | solution.py:136
  427.3 1.5 copy.96
  428.8 3.2 copy.97
  (137 shorter events, 44.7 us)
Async XLA Ops:
  7.2 2.7 copy-start
  7.2 2.5 copy-start.27
  7.2 2.5 copy-start.24
  7.2 2.6 copy-start.28
  9.7 2.2 copy-start.3
  9.8 5.0 %copy-start.18 = (f32[1536]{0:T(1024)}, f32[1536]{0:T(1024)S(1)}, u32[]{:S(2)}) copy-start(f32[1536]{0:T(1024)S(1)} %select_reduce_fusion) | copy-start | bytes 18436
  9.9 4.2 copy-start.19
  11.9 2.1 copy-start.1
  14.1 0.8 copy-start.20
  14.1 0.8 copy-start.21
  14.1 1.5 copy-start.2
  14.1 1.8 copy-start.25
  14.9 0.6 copy-start.16
  14.9 27.6 %copy-start.4 = (f32[3,32,1536]{2,1,0:T(8,128)S(1)}, f32[3,32,1536]{2,1,0:T(8,128)}, u32[]{:S(2)}) copy-start(f32[3,32,1536]{2,1,0:T(8,128)} %param.30) | copy-start | bytes 1769476
  16.0 0.6 copy-start.26
  18.8 19.3 %all-to-all-start = ((f32[8,1,768]{2,1,0:T(1,128)}), f32[8,1,768]{2,1,0:T(1,128)}, u32[]{:S(2)}, u32[]{:S(2)}) async-start(f32[8,1,768]{2,1,0:T(1,128)} %reshape.288), calls=%async_computation | async-start | bytes 49152 | tf_op jit(solution)/shard_map/all_to_all | solution.py:104
  42.5 1.8 copy-start.11
  42.5 23.0 %copy-start.22 = (s32[192,1]{0,1:T(1,128)S(1)}, s32[192,1]{0,1:T(1,128)}, u32[]{:S(2)}) copy-start(s32[192,1]{0,1:T(1,128)} %compare_select_fusion.2) | copy-start | bytes 2308
  48.2 16.5 %all-to-all-start.1 = ((f32[8,1,768]{2,1,0:T(1,128)}), f32[8,1,768]{2,1,0:T(1,128)S(1)}, u32[]{:S(2)}, u32[]{:S(2)}) async-start(f32[8,1,768]{2,1,0:T(1,128)} %reshape.290), calls=%async_computation.1 | async-start | bytes 49152 | tf_op jit(solution)/shard_map/all_to_all | solution.py:104
  67.9 1.4 copy-start.12
  67.9 28.3 %copy-start.6 = (f32[32,1536]{1,0:T(8,128)S(1)}, f32[32,1536]{1,0:T(8,128)}, u32[]{:S(2)}) copy-start(f32[32,1536]{1,0:T(8,128)} %param.31) | copy-start | bytes 589828
  67.9 28.3 %copy-start.13 = (f32[1536]{0:T(1024)S(1)}, f32[1536]{0:T(1024)}, u32[]{:S(2)}) copy-start(f32[1536]{0:T(1024)} %get-tuple-element.46) | copy-start | bytes 18436
  68.0 28.3 %copy-start.14 = (f32[1536]{0:T(1024)S(1)}, f32[1536]{0:T(1024)}, u32[]{:S(2)}) copy-start(f32[1536]{0:T(1024)} %get-tuple-element.50) | copy-start | bytes 18436
  73.3 17.8 %all-to-all-start.2 = ((f32[8,1,768]{2,1,0:T(1,128)}), f32[8,1,768]{2,1,0:T(1,128)S(1)}, u32[]{:S(2)}, u32[]{:S(2)}) async-start(f32[8,1,768]{2,1,0:T(1,128)} %reshape.292), calls=%async_computation.2 | async-start | bytes 49152 | tf_op jit(solution)/shard_map/all_to_all | solution.py:104
  97.3 0.7 copy-start.7
  97.3 26.1 %copy-start.5 = (f32[32,1536]{1,0:T(8,128)S(1)}, f32[32,1536]{1,0:T(8,128)}, u32[]{:S(2)}) copy-start(f32[32,1536]{1,0:T(8,128)} %get-tuple-element.45) | copy-start | bytes 589828
  103.3 13.4 %all-to-all-start.3 = ((f32[8,1,768]{2,1,0:T(1,128)}), f32[8,1,768]{2,1,0:T(1,128)}, u32[]{:S(2)}, u32[]{:S(2)}) async-start(f32[8,1,768]{2,1,0:T(1,128)} %reshape.294), calls=%async_computation.3 | async-start | bytes 49152 | tf_op jit(solution)/shard_map/all_to_all | solution.py:122
  126.6 0.7 copy-start.9
  132.7 12.7 %all-to-all-start.4 = ((f32[8,1,768]{2,1,0:T(1,128)}), f32[8,1,768]{2,1,0:T(1,128)}, u32[]{:S(2)}, u32[]{:S(2)}) async-start(f32[8,1,768]{2,1,0:T(1,128)} %reshape.296), calls=%async_computation.4 | async-start | bytes 49152 | tf_op jit(solution)/shard_map/all_to_all | solution.py:122
  156.3 16.9 %copy-start.17 = (f32[1536]{0:T(1024)S(1)}, f32[1536]{0:T(1024)}, u32[]{:S(2)}) copy-start(f32[1536]{0:T(1024)} %copy-done.16) | copy-start | bytes 18436
  158.0 12.2 %all-to-all-start.5 = ((f32[8,1,768]{2,1,0:T(1,128)}), f32[8,1,768]{2,1,0:T(1,128)S(1)}, u32[]{:S(2)}, u32[]{:S(2)}) async-start(f32[8,1,768]{2,1,0:T(1,128)} %reshape.298), calls=%async_computation.5 | async-start | bytes 49152 | tf_op jit(solution)/shard_map/all_to_all | solution.py:122
  163.5 49.5 %all-reduce.11.cloned.1.call-start = ((), (), s32[]{:S(2)}) async-start(), calls=%async_computation.6 | async-start | bytes 196608 | tf_op jit(solution)/shard_map/psum | solution.py:138
  174.1 6.9 %copy-start.15 = (bf16[1536,32]{0,1:T(8,128)(2,1)S(1)}, bf16[1536,32]{0,1:T(8,128)(2,1)}, u32[]{:S(2)}) copy-start(bf16[1536,32]{0,1:T(8,128)(2,1)} %param.16) | copy-start | bytes 294916
  174.1 38.9 %copy-start.23 = (f32[768]{0:T(1024)S(1)}, f32[768]{0:T(1024)}, u32[]{:S(2)}) copy-start(f32[768]{0:T(1024)} %convert_element_type.30) | copy-start | bytes 9220
  174.2 38.9 %copy-start.29 = (f32[768]{0:T(1024)S(1)}, f32[768]{0:T(1024)}, u32[]{:S(2)}) copy-start(f32[768]{0:T(1024)} %param.18) | copy-start | bytes 9220
  182.2 112.8 %all-reduce.13.cloned.1.call-start = ((), (), s32[]{:S(2)}) async-start(), calls=%async_computation.7 | async-start | bytes 196608 | tf_op jit(solution)/shard_map/psum | solution.py:137
  213.0 7.8 %copy-start.8 = (f32[32,1536]{1,0:T(8,128)S(1)}, f32[32,1536]{1,0:T(8,128)}, u32[]{:S(2)}) copy-start(f32[32,1536]{1,0:T(8,128)} %copy-done.7) | copy-start | bytes 589828
  213.0 7.8 %copy-start.10 = (f32[32,1536]{1,0:T(8,128)S(1)}, f32[32,1536]{1,0:T(8,128)}, u32[]{:S(2)}) copy-start(f32[32,1536]{1,0:T(8,128)} %copy-done.9) | copy-start | bytes 589828
  213.0 214.3 %all-reduce.15.cloned.1.call-start = ((), (), s32[]{:S(2)}) async-start(), calls=%async_computation.8 | async-start | bytes 4718592 | tf_op jit(solution)/shard_map/psum | solution.py:136
Sparse Core Ops, SparseCore 0:
  182.3 30.5 all-reduce.10
  216.7 69.4 all-reduce.12
  293.2 133.9 all-reduce.14
